TPU v7x, 512 devices: a whole 4x8x8 slice. The times are simulated.
512 devices in a mesh: ctx: 64 (over y_lo, z, core), head: 8 (over y_hi, x).
Axes of the slice: x: 4, y: 8 (y_hi: 2, y_lo: 4; y = y_hi * 4 + y_lo), z: 8, core: 2. Of those that a mesh axis runs over, the one named last changes fastest.
Arguments:
- streams: bfloat16 [8192, 8, 1024], P(('ctx', 'head'))
- steps: bfloat16 [8192, 8, 4], P(('ctx', 'head')), may hold values from -1 to 2, as said below
- skip_d: float32 [16], P('head'), may hold values from 0.5 to 2
- ssm_gain: float32 [1024], P('head'), may hold values from 0.1 to 1.9
- w_out: bfloat16 [3072, 2560], P('head'), may hold values from -0.109375 to 0.109375
Outputs:
- mixed: bfloat16 [8192, 2560], P(('ctx', 'head'))
Inputs may be any that keep to these rules, and one draw needn't show every extreme that they name: `steps`: the first 2 entries of a row are step sizes of 0.5 to 2; the last 2 are logarithms of decay factors, never positive.
All inputs are finite; a program needn't handle non-finite values.
Results may differ from a plain program's by a relative error of at most 0.017.
Values may be sent and summed in bfloat16 or wider, within the bound.
A program may use at most 64 MiB of HBM per device.

v0:
```python
import math

import jax
import jax.numpy as jnp
from jax import lax
from jax.sharding import PartitionSpec as P

HD = 128
HQ_DEV = 2
SH = 2
HP = 64
NST = 128


def entering(array, axis, combine, identity, reverse):
    peers, position = (lax.axis_size(axis), lax.axis_index(axis))
    everything = jax.tree.map(lambda part: lax.all_gather(part, axis), array)
    start = jax.tree.map(
        lambda part, zero: jnp.broadcast_to(jnp.asarray(zero, part.dtype), part.shape),
        array,
        identity,
    )

    def lap(k, before):
        at = peers - 1 - k if reverse else k
        reached = at > position if reverse else at < position
        new = combine(before, jax.tree.map(lambda part: part[at], everything))
        return jax.tree.map(lambda a, b: jnp.where(reached, a, b), new, before)

    return lax.fori_loop(0, peers, lap, start)


def combine_states(earlier, later):
    return (earlier[0] * later[0], later[0][:, None, None] * earlier[1] + later[1])


def absorb(running, q_rows, q_pos, key_block, value_block, key_pos):
    highest, totals, weighted = running
    scores = jnp.einsum("rd,kd->rk", q_rows, key_block, preferred_element_type=jnp.float32) * (
        1.0 / math.sqrt(q_rows.shape[1])
    )
    visible = key_pos[None, :] <= q_pos[:, None]
    fresh = jnp.maximum(highest, jnp.max(jnp.where(visible, scores, -1e30), axis=1))
    probs = jnp.where(visible, jnp.exp(scores - fresh[:, None]), 0.0)
    shrink = jnp.exp(highest - fresh)
    totals = totals * shrink + jnp.sum(probs, axis=1)
    weighted = weighted * shrink[:, None] + jnp.dot(
        probs.astype(jnp.bfloat16), value_block, preferred_element_type=jnp.float32
    )
    return (fresh, totals, weighted)


def body(streams, steps, skip_d, ssm_gain, w_out):
    got_streams, got_steps = (
        lax.all_to_all(streams, "head", split_axis=1, concat_axis=0, tiled=True),
        lax.all_to_all(steps, "head", split_axis=1, concat_axis=0, tiled=True),
    )
    features = got_streams[:, 0, :]
    step_vals = got_steps[:, 0, :].astype(jnp.float32)
    block_rows = features.shape[0]
    half_rows = block_rows // 2
    own_block = lax.axis_index("ctx")
    cycle_size = lax.axis_size("ctx")
    q_width = HQ_DEV * HD
    group_rows = HQ_DEV * half_rows
    queries = (
        features[:, :q_width]
        .reshape(2, half_rows, HQ_DEV, HD)
        .transpose(0, 2, 1, 3)
        .reshape(2, group_rows, HD)
    )
    spans = jnp.arange(half_rows, dtype=jnp.int32)
    early_pos = own_block * half_rows + spans
    late_pos = (2 * cycle_size - 1 - own_block) * half_rows + spans
    q_pos = jnp.stack([jnp.tile(early_pos, HQ_DEV), jnp.tile(late_pos, HQ_DEV)])
    keys = features[:, q_width : q_width + HD]
    values = features[:, q_width + HD : q_width + 2 * HD]
    start_run = (
        jnp.full((2, group_rows), -1e30, jnp.float32),
        jnp.zeros((2, group_rows), jnp.float32),
        jnp.zeros((2, group_rows, HD), jnp.float32),
    )
    key_part = lax.all_gather(keys, "ctx", axis=0, tiled=True)
    total_rows = key_part.shape[0]
    span_rows = math.gcd(total_rows, 2048)
    key_ids = jnp.arange(total_rows, dtype=jnp.int32)
    shard_id = key_ids // block_rows
    within = key_ids % block_rows
    key_pos = jnp.where(
        within < half_rows,
        shard_id * half_rows + within,
        (2 * cycle_size - 1 - shard_id) * half_rows + within - half_rows,
    )
    count = total_rows // span_rows
    blocks = (
        key_part.reshape(count, span_rows, HD),
        lax.all_gather(values, "ctx", axis=0, tiled=True).reshape(count, span_rows, HD),
        key_pos.reshape(count, span_rows),
    )
    flat_q = queries.reshape(2 * group_rows, HD)
    flat_pos = q_pos.reshape(2 * group_rows)
    flat_run = (
        start_run[0].reshape(2 * group_rows),
        start_run[1].reshape(2 * group_rows),
        start_run[2].reshape(2 * group_rows, HD),
    )

    def absorb_block(inner_run, items):
        key_blk, value_blk, pos_blk = items
        return (absorb(inner_run, flat_q, flat_pos, key_blk, value_blk, pos_blk), None)

    flat_run = lax.scan(absorb_block, flat_run, blocks)[0]
    attn_out = (
        flat_run[2].reshape(2, group_rows, HD) / flat_run[1].reshape(2, group_rows)[:, :, None]
    ).astype(jnp.bfloat16)
    attn_out = (
        attn_out.reshape(2, HQ_DEV, half_rows, HD)
        .transpose(0, 2, 1, 3)
        .reshape(block_rows, q_width)
    )
    lead = q_width + 2 * HD
    ssm_width = SH * HP
    ssm_in = features[:, lead : lead + ssm_width].astype(jnp.float32).reshape(2, half_rows, SH, HP)
    gate_z = (
        features[:, lead + ssm_width : lead + 2 * ssm_width]
        .astype(jnp.float32)
        .reshape(2, half_rows, ssm_width)
    )
    b_proj = features[:, lead + 2 * ssm_width : lead + 2 * ssm_width + NST].reshape(
        2, half_rows, NST
    )
    c_proj = features[:, lead + 2 * ssm_width + NST :].reshape(2, half_rows, NST)
    step_size = step_vals[:, :SH].reshape(2, half_rows, SH)
    cumulative = jnp.cumsum(step_vals[:, SH:].reshape(2, half_rows, SH), axis=1)
    products = jnp.einsum("itn,isn->its", c_proj, b_proj, preferred_element_type=jnp.float32)
    lower_tri = spans[:, None] >= spans[None, :]
    gaps = cumulative[:, :, None, :] - cumulative[:, None, :, :]
    mixing = (
        jnp.exp(jnp.where(lower_tri[None, :, :, None], gaps, -1e30))
        * products[..., None]
        * step_size[:, None, :, :]
    )
    intra = jnp.einsum("itsh,ishp->ithp", mixing, ssm_in, precision=lax.Precision.HIGHEST)
    to_end = jnp.exp(cumulative[:, -1:, :] - cumulative) * step_size
    pieces = jnp.einsum(
        "ish,ishp,isn->ihpn",
        to_end,
        ssm_in,
        b_proj.astype(jnp.float32),
        precision=lax.Precision.HIGHEST,
    )
    span_decay = jnp.exp(cumulative[:, -1, :])
    early_piece = (span_decay[0], pieces[0])
    late_piece = (span_decay[1], pieces[1])
    identity = (jnp.ones((SH,), jnp.float32), jnp.zeros((SH, HP, NST), jnp.float32))
    early_carry = entering(early_piece, "ctx", combine_states, identity, False)
    through_early = combine_states(early_carry, early_piece)
    at_end = own_block == cycle_size - 1
    joined = combine_states(through_early, late_piece)
    feed = (
        jnp.where(at_end, joined[0], late_piece[0]),
        jnp.where(at_end, joined[1], late_piece[1]),
    )
    late_carry = entering(feed, "ctx", combine_states, identity, True)
    late_state = jnp.where(at_end, through_early[1], late_carry[1])
    carries = jnp.stack([early_carry[1], late_state])
    inter = jnp.exp(cumulative)[..., None] * jnp.einsum(
        "itn,ihpn->ithp", c_proj.astype(jnp.float32), carries, precision=lax.Precision.HIGHEST
    )
    ssm_y = intra + inter + skip_d[None, None, :, None] * ssm_in
    gated = ssm_y.reshape(2, half_rows, ssm_width) * jax.nn.silu(gate_z)
    mean_sq = jnp.mean(gated * gated, axis=-1, keepdims=True)
    normalized_input = (
        (gated * lax.rsqrt(mean_sq + 1e-05) * ssm_gain[None, None, :])
        .astype(jnp.bfloat16)
        .reshape(block_rows, ssm_width)
    )
    combined = jnp.concatenate([attn_out, normalized_input], axis=1)
    return lax.psum_scatter(
        jnp.dot(combined, w_out, preferred_element_type=jnp.float32).astype(jnp.bfloat16),
        "head",
        scatter_dimension=0,
        tiled=True,
    )


def solution(mesh):
    return jax.shard_map(
        body,
        mesh=mesh,
        in_specs=(
            P(("ctx", "head"), None, None),
            P(("ctx", "head"), None, None),
            P("head"),
            P("head"),
            P("head", None),
        ),
        out_specs=P(("ctx", "head"), None),
        check_vma=False,
    )
```

profile of v0, /device:TPU:2, one launch (start us, length us, event | category | flops | bytes accessed | tf_op | source)
XLA Modules:
  0.0 718.2 jit_solution(15982600973743935457)
XLA Ops:
  6.5 10.2 %all-to-all-start.1 = ((bf16[16,8,4]{0,2,1:T(4,128)(2,1)}), bf16[16,8,4]{0,2,1:T(4,128)(2,1)S(1)}, u32[]{:S(2)}, u32[]{:S(2)}) async-start(bf16[16,8,4]{0,2,1:T(4,128)(2,1)} %param.12), calls=%async_computation.1 | async-start | bytes 16384 | tf_op jit(solution)/shard_map/all_to_all | solution.py:56
  16.8 1.8 copy.70
  18.6 6.8 all-to-all-done.1
  25.4 4.8 all-to-all-start
  30.7 9.0 %all-to-all-done = bf16[16,8,1024]{2,0,1:T(8,128)(2,1)S(1)} async-done(((bf16[16,8,1024]{2,0,1:T(8,128)(2,1)}), bf16[16,8,1024]{2,0,1:T(8,128)(2,1)S(1)}, u32[]{:S(2)}, u32[]{:S(2)}) %all-to-all-start) | async-done | bytes 262176 | tf_op jit(solution)/shard_map/all_to_all | solution.py:55
  42.3 82.7 %all-gather.2 = f32[64,1,2]{2,1,0:T(1,128)S(1)} all-gather(f32[1,1,2]{2,1,0:T(1,128)S(1)} %get-tuple-element.457), channel_id=1, replica_groups=mesh['ctx'=64,'head'=8] {'ctx'}, dimensions={0}, use_global_device_ids=true | all-gather | bytes 520 | tf_op jit(solution)/shard_map/all_gather | solution.py:17
  125.1 35.9 %all-gather.12.cloned.1.call-done = f32[64,2,64,128]{3,2,1,0:T(8,128)} async-done(((f32[1,2,64,128]{3,2,1,0:T(8,128)}), f32[64,2,64,128]{3,2,1,0:T(8,128)}) %all-gather.12.cloned.1.call-update) | async-done | bytes 4194320 | tf_op jit(solution)/shard_map/all_gather | solution.py:17
  161.0 60.1 %while.48 = (s32[]{:T(128)}, f32[2]{0:T(128)S(1)}, f32[2,64,128]{2,1,0:T(8,128)S(1)}, s32[]{:T(128)}, f32[64,2]{1,0:T(8,128)S(1)}, /*index=5*/f32[64,2,64,128]{3,2,1,0:T(8,128)}, s32[]{:T(128)}, s32[]{:T(128)}) while((s32[]{:T(128)}, f32[2]{0:T(128)S(1)}, f32[2,64,128]{2,1,0:T(8,128)S(1)}, s32[]{:T(128)}, f32[64,2]{1,0:T(8,128)S(1)}, ...), condition=%wide.region_6.7_spmd.clone, body=%wide.region_5.6_spmd.clone.sunk | while | flops 65546 | bytes 196763 | solution.py:30
  198.6 0.9 fusion.75
  201.4 0.9 fusion.75
  206.1 0.9 fusion.75
  216.4 0.9 fusion.75
  222.2 1.3 dynamic-slice
  224.8 54.8 %all-gather.8.cloned.1.call-done = bf16[8192,128]{1,0:T(8,128)(2,1)} async-done(((bf16[128,128]{1,0:T(8,128)(2,1)}), bf16[8192,128]{1,0:T(8,128)(2,1)}) %all-gather.8.cloned.1.call-update) | async-done | bytes 2097168 | tf_op jit(solution)/shard_map/all_gather | solution.py:83
  279.6 118.3 %all-gather.10.cloned.1.call-done = bf16[8192,128]{1,0:T(8,128)(2,1)} async-done(((bf16[128,128]{1,0:T(8,128)(2,1)}), bf16[8192,128]{1,0:T(8,128)(2,1)}) %all-gather.10.cloned.1.call-update) | async-done | bytes 2097168 | tf_op jit(solution)/shard_map/all_gather | solution.py:97
  397.8 28.4 %while.47 = (s32[]{:T(128)}, f32[256]{0:T(256)S(1)}, f32[256]{0:T(256)S(1)}, f32[256,128]{1,0:T(8,128)S(1)}, s32[4,2048]{1,0:T(4,128)S(1)}, /*index=5*/s32[2,128...) while((s32[]{:T(128)}, f32[256]{0:T(256)S(1)}, ...), condition=%wide.region_3.4_spmd.clone, body=%wide.region_0.3_spmd.clone.sunk | while | flops 274826496 | bytes 16117913 | solution.py:112
  397.9 2.9 fusion.71
  400.8 1.9 fusion.73
  403.0 1.9 convolution_add_fusion.2
  405.0 2.9 fusion.71
  407.9 1.9 fusion.73
  410.1 1.9 convolution_add_fusion.2
  412.1 2.9 fusion.71
  415.0 1.9 fusion.73
  417.2 1.9 convolution_add_fusion.2
  419.2 2.9 fusion.71
  422.1 1.9 fusion.73
  424.4 1.9 convolution_add_fusion.2
  426.7 136.0 %all-reduce = f32[128]{0:T(128)S(1)} all-reduce(f32[128]{0:T(128)S(1)} %fusion.44), channel_id=2, replica_groups=mesh['ctx'=64,'head'=8] {'ctx'}, use_global_device_ids=true, to_apply=%add | all-reduce | flops 128 | bytes 1024
  562.9 61.0 %while.49 = (s32[]{:T(128)}, f32[2,64,128]{2,1,0:T(8,128)S(1)}, s32[]{:T(128)}, f32[64,2]{1,0:T(8,128)S(1)}, f32[64,2,64,128]{3,2,1,0:T(8,128)}, /*index=5*/s32[]{:T(128)}, s32[]{:T(128)}, s32[]{:T(128)}, s32[]{:T(128)}) while((s32[]{:T(128)}, f32[2,64,128]{2,1,0:T(8,128)S(1)}, s32[]{:T(128)}, f32[64,2]{1,0:T(8,128)S(1)}, ...), condition=%wide.region_8.9_spmd.clone, body=%wide.region_7.8_spmd.clone.sunk | while | flops 65544 | bytes 196799 | solution.py:30
  625.0 1.4 convolution_convert_fusion
  626.4 85.3 %reduce-scatter.2.cloned.1.call-done = bf16[16,2560]{1,0:T(8,128)(2,1)} async-done(((bf16[128,2560]{1,0:T(8,128)(2,1)}), bf16[16,2560]{1,0:T(8,128)(2,1)}) %reduce-scatter.2.cloned.1.call-update) | async-done | bytes 81936 | tf_op jit(solution)/shard_map/reduce_scatter | solution.py:179
  (350 shorter events, 123.7 us)
Async XLA Ops:
  6.5 618.4 %copy-start = (bf16[384,2560]{1,0:T(8,128)(2,1)S(1)}, bf16[384,2560]{1,0:T(8,128)(2,1)}, u32[]{:S(2)}) copy-start(bf16[384,2560]{1,0:T(8,128)(2,1)} %param.15) | copy-start | bytes 5898244
  6.5 18.9 %all-to-all-start.1 = ((bf16[16,8,4]{0,2,1:T(4,128)(2,1)}), bf16[16,8,4]{0,2,1:T(4,128)(2,1)S(1)}, u32[]{:S(2)}, u32[]{:S(2)}) async-start(bf16[16,8,4]{0,2,1:T(4,128)(2,1)} %param.12), calls=%async_computation.1 | async-start | bytes 16384 | tf_op jit(solution)/shard_map/all_to_all | solution.py:56
  25.4 14.3 %all-to-all-start = ((bf16[16,8,1024]{2,0,1:T(8,128)(2,1)}), bf16[16,8,1024]{2,0,1:T(8,128)(2,1)S(1)}, u32[]{:S(2)}, u32[]{:S(2)}) async-start(bf16[16,8,1024]{2,0,1:T(8,128)(2,1)} %copy.70), calls=%async_computation | async-start | bytes 524288 | tf_op jit(solution)/shard_map/all_to_all | solution.py:55
  30.2 130.8 %all-gather.12.cloned.1.call-start = ((), (), s32[]{:S(2)}) async-start(), calls=%async_computation.5 | async-start | bytes 4259840 | tf_op jit(solution)/shard_map/all_gather | solution.py:17
  41.5 238.1 %all-gather.8.cloned.1.call-start = ((), (), s32[]{:S(2)}) async-start(), calls=%async_computation.3 | async-start | bytes 2129920 | tf_op jit(solution)/shard_map/all_gather | solution.py:83
  42.2 355.6 %all-gather.10.cloned.1.call-start = ((), (), s32[]{:S(2)}) async-start(), calls=%async_computation.4 | async-start | bytes 2129920 | tf_op jit(solution)/shard_map/all_gather | solution.py:97
  125.0 437.8 %all-gather.14.cloned.1.call-start = ((), (), s32[]{:S(2)}) async-start(), calls=%async_computation.7 | async-start | bytes 4259840 | tf_op jit(solution)/shard_map/all_gather | solution.py:17
  221.9 489.8 %reduce-scatter.2.cloned.1.call-start = ((), (), s32[]{:S(2)}) async-start(), calls=%async_computation.6 | async-start | bytes 737280 | tf_op jit(solution)/shard_map/reduce_scatter | solution.py:179
  400.8 2.2 copy-start.1
  407.9 2.2 copy-start.1
  415.0 2.2 copy-start.1
  422.1 2.2 copy-start.1
  426.3 197.9 %copy-start.3 = (f32[2]{0:T(128)S(1)}, f32[2]{0:T(128)}, u32[]{:S(2)}) copy-start(f32[2]{0:T(128)} %param.13) | copy-start | bytes 28
  426.3 198.6 %copy-start.2 = (f32[128]{0:T(128)S(1)}, f32[128]{0:T(128)}, u32[]{:S(2)}) copy-start(f32[128]{0:T(128)} %param.14) | copy-start | bytes 1540
Sparse Core Ops, SparseCore 0:
  41.6 119.3 all-gather.11
  163.1 116.4 all-gather.7
  281.7 116.0 all-gather.9
  399.9 118.3 all-gather.13
  626.5 85.0 reduce-scatter.1
where the time goes:
time: 725 us; the launch traced here: 718 us
  waiting for transfers between devices  311 us (43%)
  blocking collectives  219 us (30%)
  other arithmetic  129 us (18%)
  matrix products  21.6 us (3%)
  starting transfers between devices  15.2 us (2%)
  between operations  14 us (2%)
  local copies, waits for them, and re-layouts  7.41 us (1%)
    unnamed x1, blocking collectives  136 us
    select_n x192, other arithmetic, lap(): return jax.tree.map(lambda a, b: jnp.where(reached, a, b), new, before)  119 us
    all_gather x1, waiting for transfers between devices, body(): lax.all_gather(values, 'ctx', axis=0, tiled=True)  118 us
    reduce_scatter x1, waiting for transfers between devices, body(): lax.psum_scatter(jnp.dot(combined, w_out, preferred_element_type=jnp.floa...  85.3 us
    all_gather x1, blocking collectives, entering(): everything = jax.tree.map(lambda part: lax.all_gather(part, axis), array)  82.7 us
    all_gather x1, waiting for transfers between devices, body(): key_part = lax.all_gather(keys, 'ctx', axis=0, tiled=True)  54.8 us
    all_gather x2, waiting for transfers between devices, entering(): everything = jax.tree.map(lambda part: lax.all_gather(part, axis), array)  35.9 us
  transfers between devices with their start and end apart: 7, of which 6 were waited for; matrix products, arithmetic and copies ran while one was open for 13% of the time, Pallas kernels for 0%

commit v1 on v0

v1 whole, which is shorter than its diff:
```python
import functools
import math

import jax
import jax.numpy as jnp
from jax import lax
from jax.experimental import pallas as pl
from jax.experimental.pallas import tpu as pltpu
from jax.sharding import PartitionSpec as P

HD = 128
HP = 64
NST = 128
ROWS = 16
DOUT = 2560
N_YLO, N_Z, N_CORE, N_YHI, N_X = 4, 8, 2, 2, 4
MESH = pl.DeviceIdType.MESH
F32, BF16 = jnp.float32, jnp.bfloat16
NEG = -1e30
CUTS = 5


def nt_dot(a, b):
    return lax.dot_general(a, b, (((1,), (1,)), ((), ())), preferred_element_type=F32)


def nn_dot(a, b):
    return jnp.dot(a, b, preferred_element_type=F32)


def kernel(
    sizes,
    x_ref,
    skip_ref,
    gain_ref,
    w_hbm,
    out_ref,
    kv,
    qraw,
    q,
    feat,
    w_ref,
    vt,
    stat,
    acc,
    st_out,
    st_in,
    gt_out,
    gt,
    reach,
    carry_out,
    carry_in,
    o_out,
    os_out,
    o_in,
    os_in,
    comb,
    prod,
    rsx,
    red_out,
    keep,
    rsy,
    local_sem,
    a_send,
    a_recv,
    kv_send,
    kv_recv,
    fw_send,
    fw_recv,
    q_send,
    q_recv,
    st_send,
    st_recv,
    gt_send,
    gt_recv,
    ca_send,
    ca_recv,
    o_send,
    o_recv,
    x_send,
    x_recv,
    y_send,
    y_recv,
):
    ny, nz, nx = sizes
    nh, nj = 2 * nx, 2 * nz
    tok = nh * ROWS
    half = tok // 2
    group = 2 * half
    part = 128 // nj
    scale = math.log2(math.e) / math.sqrt(HD)
    order = [0]
    for d in range(1, nz // 2 + 1):
        order += [d] if 2 * d == nz else [d, nz - d]

    c, h = lax.axis_index("ctx"), lax.axis_index("head")
    a, j = c // nj, c % nj
    z, core = j // 2, j % 2
    yh, xx = h // nx, h % nx
    sends = []

    def push(src, dst, send_sem, recv_sem, device):
        copy = pltpu.make_async_remote_copy(
            src_ref=src,
            dst_ref=dst,
            send_sem=send_sem,
            recv_sem=recv_sem,
            device_id=device,
            device_id_type=MESH,
        )
        copy.start()
        sends.append(copy)

    def landed(dst, recv_sem):
        pltpu.make_async_copy(dst, dst, recv_sem).wait()

    def at_ylo(i):
        return (((a + i) % ny) * nj + j, h)

    def at_j(i):
        return (a * nj + (j + i) % nj, h)

    def at_z(d):
        return (a * nj + ((z + d) % nz) * 2 + core, h)

    def at_head(i):
        return (c, (h + i) % nh)

    def at_x(i):
        return (c, yh * nx + (xx + i) % nx)

    sibling = (a * nj + z * 2 + (1 - core), h)
    across = (c, (1 - yh) * nx + xx)

    w_copy = pltpu.make_async_copy(w_hbm, w_ref, local_sem.at[3])
    places = [
        (slice(256, 512), lambda s: kv.at[s // nx, 0, pl.ds(pl.multiple_of((s % nx) * ROWS, ROWS), ROWS), :]),
        (slice(0, 256), lambda s: qraw.at[pl.ds(pl.multiple_of(s * ROWS, ROWS), ROWS), :]),
        (slice(512, 1152), lambda s: feat.at[pl.ds(pl.multiple_of(s * ROWS, ROWS), ROWS), :]),
    ]
    own = []
    for n, (columns, place) in enumerate(places):
        copy = pltpu.make_async_copy(x_ref.at[h, :, columns], place(h), local_sem.at[n])
        copy.start()
        own.append(copy)
    w_copy.start()

    barrier = pltpu.get_barrier_semaphore()
    peers = [at_head(i) for i in range(1, nh)] + [at_j(i) for i in range(1, nj)] + [at_ylo(i) for i in range(1, ny)]
    for peer in peers:
        pl.semaphore_signal(barrier, inc=1, device_id=peer, device_id_type=MESH)
    pl.semaphore_wait(barrier, len(peers))

    for n, (columns, place) in enumerate(places):
        for i in range(1, nh):
            g = (h + i) % nh
            push(x_ref.at[g, :, columns], place(h), a_send.at[n, i], a_recv.at[n, i], at_head(i))

    def rows_in(n):
        own[n].wait()
        for i in range(1, nh):
            landed(places[n][1]((h + nh - i) % nh), a_recv.at[n, i])

    rows_in(0)
    push(kv.at[:, 0], kv.at[:, 1], fw_send.at[0], fw_recv.at[0], sibling)
    for e in range(1, nz):
        d = (nz - order[e]) % nz
        push(kv.at[:, 0], kv.at[:, 2 * e], kv_send.at[e], kv_recv.at[e], at_z(d))

    rows_in(1)
    for i in range(2):
        for n in range(2):
            q[0, i, n * half : (n + 1) * half, :] = qraw[i * half : (i + 1) * half, n * HD : (n + 1) * HD]
    for i in range(1, ny):
        push(q.at[0], q.at[ny - i], q_send.at[i], q_recv.at[i], at_ylo(i))

    rows_in(2)
    x_in = feat[:, 0:128]
    b_in = feat[:, 256:384]
    c_in = feat[:, 384:512]
    st = feat[:, 512:640]
    row_id = lax.broadcasted_iota(jnp.int32, (tok, tok), 0)
    col_id = lax.broadcasted_iota(jnp.int32, (tok, tok), 1)
    lower = (col_id <= row_id) & ((row_id < half) == (col_id < half))
    cum = nn_dot(jnp.where(lower, 1.0, 0.0).astype(BF16), st)
    st_f = st.astype(F32)
    lane = lax.broadcasted_iota(jnp.int32, (tok, 128), 1)
    early_row = lax.broadcasted_iota(jnp.int32, (tok, 128), 0) < half
    first_head = lane < HP
    total_e, total_l = cum[half - 1 : half, :], cum[tok - 1 : tok, :]
    to_end = jnp.exp(jnp.where(early_row, total_e, total_l) - cum)
    weigh = jnp.where(first_head, to_end[:, 2:3] * st_f[:, 0:1], to_end[:, 3:4] * st_f[:, 1:2])
    x_f = x_in.astype(F32)
    xs_t = (x_f * weigh).T
    early_lane = lax.broadcasted_iota(jnp.int32, (128, tok), 1) < half
    piece_e = nn_dot(jnp.where(early_lane, xs_t, 0.0).astype(BF16), b_in)
    piece_l = nn_dot(jnp.where(early_lane, 0.0, xs_t).astype(BF16), b_in)
    st_out[:, 0:part, :] = piece_e.reshape(nj, part, NST)
    st_out[:, part : 2 * part, :] = piece_l.reshape(nj, part, NST)
    upper_rows = lax.broadcasted_iota(jnp.int32, (8, 128), 0) < 4
    for s in range(2):
        tile = jnp.exp(
            jnp.where(
                upper_rows,
                jnp.broadcast_to(total_e[:, 2 + s : 3 + s], (8, 128)),
                jnp.broadcast_to(total_l[:, 2 + s : 3 + s], (8, 128)),
            )
        )
        st_out[s * (nj // 2) : (s + 1) * (nj // 2), 2 * part :, :] = jnp.broadcast_to(tile[None], (nj // 2, 8, 128))
    for i in range(1, nj):
        push(st_out.at[(j + i) % nj], st_in.at[j], st_send.at[i], st_recv.at[i], at_j(i))
    st_in[j] = st_out[j]

    cum_t, st_t = cum.T, st_f.T
    pairs = nt_dot(c_in, b_in)
    within = []
    for s in range(2):
        gap = jnp.where(lower, cum[:, 2 + s : 3 + s] - cum_t[2 + s : 3 + s, :], NEG)
        mix = jnp.exp(gap) * pairs * st_t[s : s + 1, :]
        within.append(nn_dot(mix.astype(BF16), x_in))
    skip = jnp.where(first_head, skip_ref[0], skip_ref[1])
    intra = jnp.where(first_head, within[0], within[1]) + skip * x_f

    def forward(e):
        landed(kv.at[:, 2 * e], kv_recv.at[e])
        push(kv.at[:, 2 * e], kv.at[:, 2 * e + 1], fw_send.at[e], fw_recv.at[e], sibling)

    key_row = lax.broadcasted_iota(jnp.int32, (4 * half, group), 0)
    q_tok = lax.broadcasted_iota(jnp.int32, (4 * half, group), 1) % half
    picked = [None] + [jnp.where(a + i < ny, 0, 1) for i in range(1, ny)]

    def absorb(scores, values_t, lanes, first):
        top = jnp.max(scores, axis=0, keepdims=True)
        if not first:
            before = stat[0:1, lanes]
            top = jnp.maximum(top, before)
        probs = jnp.exp2(scores * scale - top * scale)
        total = jnp.sum(probs, axis=0, keepdims=True)
        added = nn_dot(values_t, probs.astype(BF16))
        if not first:
            shrink = jnp.exp2((before - top) * scale)
            total = total + stat[1:2, lanes] * shrink
            added = added + acc[:, lanes] * shrink
        stat[0:1, lanes] = top
        stat[1:2, lanes] = total
        acc[:, lanes] = added

    def attend(n):
        first = n == 0
        slots = slice(4 * n, 4 * n + 4)
        for i in range(2):
            vt[i] = kv[i, slots, :, HD : 2 * HD].reshape(4 * half, HD).T
        keys_e = kv[0, slots, :, 0:HD].reshape(4 * half, HD)
        keys_l = kv[1, slots, :, 0:HD].reshape(4 * half, HD)
        absorb(nt_dot(keys_e, q[:, 1].reshape(ny * group, HD)), vt[0], slice(0, ny * group), first)
        for i in range(1, ny):
            s = picked[i]
            at = (ny + i - 1) * group
            keys = kv[s, slots, :, 0:HD].reshape(4 * half, HD)
            absorb(nt_dot(keys, q[i, s]), vt[s], slice(at, at + group), first)
        block = jnp.zeros((4 * half, group), jnp.int32)
        for m in range(4):
            from_z = (z + order[2 * n + m // 2]) % nz
            from_core = core if m % 2 == 0 else 1 - core
            block = jnp.where(key_row // half == m, from_z * 2 + from_core, block)
        key_tok = key_row % half
        see_e = block * half + key_tok <= j * half + q_tok
        see_l = (nj - 1 - block) * half + key_tok <= (nj - 1 - j) * half + q_tok
        at = (2 * ny - 1) * group
        absorb(jnp.where(see_e, nt_dot(keys_e, q[0, 0]), NEG), vt[0], slice(at, at + group), first)
        at = 2 * ny * group
        absorb(jnp.where(see_l, nt_dot(keys_l, q[0, 1]), NEG), vt[1], slice(at, at + group), first)

    def chunk(n):
        for e in (2 * n, 2 * n + 1):
            landed(kv.at[:, 2 * e + 1], fw_recv.at[e])
        attend(n)

    def states_in():
        for i in range(1, nj):
            landed(st_in.at[(j + nj - i) % nj], st_recv.at[i])
        state = jnp.zeros((part, NST), F32)
        decay = jnp.ones((1, NST), F32)
        for k in range(nj):
            carry_out[k, 0:part, :] = state
            reach[k, 0:1, :] = decay
            d = st_in[k, 2 * part : 2 * part + 1, :]
            state = d * state + st_in[k, 0:part, :]
            decay = d * decay
        gt_out[0:part, :] = state
        gt_out[2 * part : 2 * part + 4, :] = jnp.broadcast_to(decay, (4, NST))
        state = jnp.zeros((part, NST), F32)
        decay = jnp.ones((1, NST), F32)
        for k in reversed(range(nj)):
            carry_out[k, part : 2 * part, :] = state
            reach[k, 1:2, :] = decay
            d = st_in[k, 2 * part + 4 : 2 * part + 5, :]
            state = d * state + st_in[k, part : 2 * part, :]
            decay = d * decay
        gt_out[part : 2 * part, :] = state
        gt_out[2 * part + 4 : 2 * part + 8, :] = jnp.broadcast_to(decay, (4, NST))
        for i in range(1, ny):
            push(gt_out, gt.at[a], gt_send.at[i], gt_recv.at[i], at_ylo(i))
        gt[a] = gt_out[...]

    def carries_out():
        for i in range(1, ny):
            landed(gt.at[(a + ny - i) % ny], gt_recv.at[i])
        enter_e = jnp.zeros((part, NST), F32)
        enter_l = jnp.zeros((part, NST), F32)
        state = jnp.zeros((part, NST), F32)
        for g in range(ny):
            enter_e = jnp.where(a == g, state, enter_e)
            state = gt[g, 2 * part : 2 * part + 1, :] * state + gt[g, 0:part, :]
        for g in reversed(range(ny)):
            enter_l = jnp.where(a == g, state, enter_l)
            state = gt[g, 2 * part + 4 : 2 * part + 5, :] * state + gt[g, part : 2 * part, :]
        for k in range(nj):
            carry_out[k, 0:part, :] += reach[k, 0:1, :] * enter_e
            carry_out[k, part : 2 * part, :] += reach[k, 1:2, :] * enter_l
        for i in range(1, nj):
            push(carry_out.at[(j + i) % nj], carry_in.at[j], ca_send.at[i], ca_recv.at[i], at_j(i))
        carry_in[j] = carry_out[j]

    chunks = nz // 2
    forward(1)
    for i in range(1, ny):
        landed(q.at[ny - i], q_recv.at[i])
    if nz > 2:
        forward(2)
    chunk(0)
    states_in()
    for n in range(1, chunks):
        forward(2 * n + 1)
        if n + 1 < chunks:
            forward(2 * n + 2)
        if n == 1:
            carries_out()
        chunk(n)
    if chunks == 1:
        carries_out()

    for i in range(1, ny):
        for n, at in enumerate((i * group, (ny + i - 1) * group)):
            o_out[i - 1, n] = acc[:, at : at + group].astype(BF16)
            os_out[i - 1, 2 * n : 2 * n + 2, :] = stat[0:2, at : at + group]
        os_out[i - 1, 4:8, :] = jnp.zeros((4, group), F32)
        push(os_out.at[i - 1], os_in.at[ny - i - 1], o_send.at[0, i], o_recv.at[0, i], at_ylo(i))
        push(o_out.at[i - 1], o_in.at[ny - i - 1], o_send.at[1, i], o_recv.at[1, i], at_ylo(i))

    for i in range(1, nj):
        landed(carry_in.at[(j + nj - i) % nj], ca_recv.at[i])
    carry_e = carry_in[:, 0:part, :].reshape(128, NST).astype(BF16)
    carry_l = carry_in[:, part : 2 * part, :].reshape(128, NST).astype(BF16)
    inter = jnp.where(early_row, nt_dot(c_in, carry_e), nt_dot(c_in, carry_l))
    ssm_y = intra + inter * jnp.exp(jnp.where(first_head, cum[:, 2:3], cum[:, 3:4]))
    gate = feat[:, 128:256].astype(F32)
    gated = ssm_y * (gate / (1.0 + jnp.exp(-gate)))
    mean_sq = jnp.mean(gated * gated, axis=1, keepdims=True)
    comb[:, 2 * HD : 3 * HD] = (gated * lax.rsqrt(mean_sq + 1e-05) * gain_ref[...]).astype(BF16)

    def unit(n):
        lanes = slice(n * group, (n + 1) * group)
        return stat[0:1, lanes], stat[1:2, lanes], acc[:, lanes]

    early, late = [unit(2 * ny - 1)], [unit(0), unit(2 * ny)]
    for i in range(1, ny):
        landed(os_in.at[ny - i - 1], o_recv.at[0, i])
        landed(o_in.at[ny - i - 1], o_recv.at[1, i])
    for i in range(1, ny):
        s = os_in[i - 1]
        late.append((s[0:1], s[1:2], o_in[i - 1, 0].astype(F32)))
        is_early = a + i >= ny
        other = o_in[i - 1, 1].astype(F32)
        early.append((jnp.where(is_early, s[2:3], NEG), s[3:4], other))
        late.append((jnp.where(is_early, NEG, s[2:3]), s[3:4], other))
    for n, parts in enumerate((early, late)):
        top = functools.reduce(jnp.maximum, [p[0] for p in parts])
        total, weighted = 0.0, 0.0
        for m, l, o in parts:
            w = jnp.exp2((m - top) * scale)
            total = total + w * l
            weighted = weighted + w * o
        attn = (weighted / total).T.astype(BF16)
        rows = slice(n * half, (n + 1) * half)
        comb[rows, 0:HD] = attn[0:half]
        comb[rows, HD : 2 * HD] = attn[half:]

    w_copy.wait()
    width = DOUT // CUTS
    for n in range(CUTS):
        share = nn_dot(comb[...], w_ref[:, n * width : (n + 1) * width]).astype(BF16)
        prod[n] = share.reshape(2, nx, ROWS, width)
        for i in range(1, nx):
            push(
                prod.at[n, :, (xx + i) % nx],
                rsx.at[n, nx - i - 1],
                x_send.at[n, i],
                x_recv.at[n, i],
                at_x(i),
            )
    for n in range(CUTS):
        for i in range(1, nx):
            landed(rsx.at[n, nx - i - 1], x_recv.at[n, i])
        mine = prod[n, yh, xx].astype(F32)
        other = prod[n, 1 - yh, xx].astype(F32)
        for i in range(nx - 1):
            mine = mine + rsx[n, i, yh].astype(F32)
            other = other + rsx[n, i, 1 - yh].astype(F32)
        red_out[n] = other.astype(BF16)
        push(red_out.at[n], rsy.at[n], y_send.at[n], y_recv.at[n], across)
        keep[n] = mine
    for n in range(CUTS):
        landed(rsy.at[n], y_recv.at[n])
        out_ref[:, n * width : (n + 1) * width] = (keep[n] + rsy[n].astype(F32)).astype(BF16)
    for copy in sends:
        copy.wait_send()


def make(sizes):
    ny, nz, nx = sizes
    nh, nj = 2 * nx, 2 * nz
    tok = nh * ROWS
    half = tok // 2
    group = 2 * half
    part = 128 // nj
    width = DOUT // CUTS
    units = 2 * ny + 1

    def body(streams, steps, skip_d, ssm_gain, w_out):
        padded = jnp.pad(steps, ((0, 0), (0, 0), (0, 128 - steps.shape[2])))
        x = jnp.concatenate([streams, padded], axis=2).transpose(1, 0, 2)
        dma = pltpu.SemaphoreType.DMA
        scratch = dict(
            kv=pltpu.VMEM((2, 2 * nz, half, 2 * HD), BF16),
            qraw=pltpu.VMEM((tok, 2 * HD), BF16),
            q=pltpu.VMEM((ny, 2, group, HD), BF16),
            feat=pltpu.VMEM((tok, 640), BF16),
            w_ref=pltpu.VMEM((3 * HD, DOUT), BF16),
            vt=pltpu.VMEM((2, HD, 4 * half), BF16),
            stat=pltpu.VMEM((8, units * group), F32),
            acc=pltpu.VMEM((HD, units * group), F32),
            st_out=pltpu.VMEM((nj, 2 * part + 8, NST), F32),
            st_in=pltpu.VMEM((nj, 2 * part + 8, NST), F32),
            gt_out=pltpu.VMEM((2 * part + 8, NST), F32),
            gt=pltpu.VMEM((ny, 2 * part + 8, NST), F32),
            reach=pltpu.VMEM((nj, 8, NST), F32),
            carry_out=pltpu.VMEM((nj, 2 * part, NST), F32),
            carry_in=pltpu.VMEM((nj, 2 * part, NST), F32),
            o_out=pltpu.VMEM((ny - 1, 2, HD, group), BF16),
            os_out=pltpu.VMEM((ny - 1, 8, group), F32),
            o_in=pltpu.VMEM((ny - 1, 2, HD, group), BF16),
            os_in=pltpu.VMEM((ny - 1, 8, group), F32),
            comb=pltpu.VMEM((tok, 3 * HD), BF16),
            prod=pltpu.VMEM((CUTS, 2, nx, ROWS, width), BF16),
            rsx=pltpu.VMEM((CUTS, nx - 1, 2, ROWS, width), BF16),
            red_out=pltpu.VMEM((CUTS, ROWS, width), BF16),
            keep=pltpu.VMEM((CUTS, ROWS, width), F32),
            rsy=pltpu.VMEM((CUTS, ROWS, width), BF16),
            local_sem=dma((4,)),
            a_send=dma((3, nh)),
            a_recv=dma((3, nh)),
            kv_send=dma((nz,)),
            kv_recv=dma((nz,)),
            fw_send=dma((nz,)),
            fw_recv=dma((nz,)),
            q_send=dma((ny,)),
            q_recv=dma((ny,)),
            st_send=dma((nj,)),
            st_recv=dma((nj,)),
            gt_send=dma((ny,)),
            gt_recv=dma((ny,)),
            ca_send=dma((nj,)),
            ca_recv=dma((nj,)),
            o_send=dma((2, ny)),
            o_recv=dma((2, ny)),
            x_send=dma((CUTS, nx)),
            x_recv=dma((CUTS, nx)),
            y_send=dma((CUTS,)),
            y_recv=dma((CUTS,)),
        )
        return pl.pallas_call(
            functools.partial(kernel, sizes),
            out_shape=jax.ShapeDtypeStruct((ROWS, DOUT), BF16),
            in_specs=[
                pl.BlockSpec(memory_space=pl.ANY),
                pl.BlockSpec(memory_space=pltpu.SMEM),
                pl.BlockSpec(memory_space=pltpu.VMEM),
                pl.BlockSpec(memory_space=pl.ANY),
            ],
            out_specs=pl.BlockSpec(memory_space=pltpu.VMEM),
            scratch_shapes=list(scratch.values()),
            compiler_params=pltpu.CompilerParams(
                collective_id=0, has_side_effects=True, vmem_limit_bytes=48 * 1024 * 1024
            ),
        )(x, skip_d, ssm_gain.reshape(1, 128), w_out)

    return body


def solution(mesh):
    return jax.shard_map(
        make((N_YLO, N_Z, N_X)),
        mesh=mesh,
        in_specs=(
            P(("ctx", "head"), None, None),
            P(("ctx", "head"), None, None),
            P("head"),
            P("head"),
            P("head", None),
        ),
        out_specs=P(("ctx", "head"), None),
        check_vma=False,
    )
```

time: 725 us -> 77.3 us (0.11)
  the two profiles are of different devices: /device:TPU:2 before, /device:TPU:8 now
where the time goes in v1:
time: 77.3 us; the launch traced here: 77.1 us
  Pallas kernels  71.6 us (93%)
  local copies, waits for them, and re-layouts  5.42 us (7%)
    pallas_call x1, Pallas kernels, body(): pl.pallas_call(functools.partial(kernel, sizes), out_shape=jax.ShapeDtype...  71.6 us
    unnamed x9, local copies, waits for them, and re-layouts  5.42 us

profile of v1, /device:TPU:8, one launch (start us, length us, event | category | flops | bytes accessed | tf_op | source)
XLA Modules:
  0.0 77.1 jit_solution(6175935268937344348)
XLA Ops:
  0.0 0.8 %copy.6 = bf16[16,8,4]{2,0,1:T(8,128)(2,1)S(1)} copy(bf16[16,8,4]{0,2,1:T(4,128)(2,1)} %param.6) | data formatting | bytes 2048 | tf_op args[1]
  0.8 1.1 %copy.7 = bf16[16,8,1024]{2,0,1:T(8,128)(2,1)S(1)} copy(bf16[16,8,1024]{2,1,0:T(8,128)(2,1)} %param.5) | data formatting | bytes 524288 | tf_op args[0]
  2.0 0.0 copy-start
  2.0 1.5 %copy-done = bf16[384,2560]{1,0:T(8,128)(2,1)S(1)} copy-done((bf16[384,2560]{1,0:T(8,128)(2,1)S(1)}, bf16[384,2560]{1,0:T(8,128)(2,1)}, u32[]{:S(2)}) %copy-start) | copy-done | bytes 1966104
  3.5 0.0 copy-start.1
  3.5 0.7 copy-done.1
  4.2 0.0 copy-start.2
  4.2 0.7 copy-done.2
  4.8 71.6 %shard_map.55 = bf16[16,2560]{1,0:T(8,128)(2,1)S(1)} custom-call(bf16[8,16,1152]{2,1,0:T(8,128)(2,1)S(1)} %fusion.2.x_ref, f32[2]{0:T(128)S(1)} %copy-done.1, f32[1,128]{1,0:T(1,128)S(1)} %bitcast.3, bf16[384,2560]{1,0:T(8,128)(2,1)S(1)} %copy-done), custom_call_target="tpu_custom_call" | custom-call | tf_op jit(solution)/shard_map/pallas_call | solution.py:482
  76.5 0.6 copy.9
  (1 shorter events, 0.0 us)
Async XLA Ops:
  2.0 1.5 %copy-start = (bf16[384,2560]{1,0:T(8,128)(2,1)S(1)}, bf16[384,2560]{1,0:T(8,128)(2,1)}, u32[]{:S(2)}) copy-start(bf16[384,2560]{1,0:T(8,128)(2,1)} %w_hbm.1) | copy-start | bytes 5898244
  3.5 0.7 copy-start.1
  4.2 0.7 copy-start.2

commit v2 on v1

v2 whole, which is shorter than its diff:
```python
import functools
import math

import jax
import jax.numpy as jnp
from jax import lax
from jax.experimental import pallas as pl
from jax.experimental.pallas import tpu as pltpu
from jax.sharding import PartitionSpec as P

HD = 128
HP = 64
NST = 128
ROWS = 16
DOUT = 2560
N_YLO, N_Z, N_CORE, N_YHI, N_X = 4, 8, 2, 2, 4
MESH = pl.DeviceIdType.MESH
F32, BF16 = jnp.float32, jnp.bfloat16
NEG = -1e30
CUTS = 2
LEAVE = (0, 1, 2, 3)
PLAN = (
    "keys0",
    "keys1",
    "queries",
    "pieces",
    "slices",
    "pass01",
    "pass02",
    "pass03",
    "pass04",
    "pass05",
    "pass06",
    "pass07",
    "intra",
    "pass11",
    "attend0",
    "pass12",
    "pass13",
    "attend1",
    "states",
    "pass14",
    "pass15",
    "attend2",
    "carries",
    "pass16",
    "pass17",
    "attend3",
)


def nt_dot(a, b):
    return lax.dot_general(a, b, (((1,), (1,)), ((), ())), preferred_element_type=F32)


def nn_dot(a, b):
    return jnp.dot(a, b, preferred_element_type=F32)


def kernel(
    sizes,
    x_ref,
    steps_hbm,
    skip_hbm,
    gain_hbm,
    w_hbm,
    out_ref,
    kv,
    qraw,
    q,
    feat,
    steps_ref,
    steps_out,
    steps_in,
    skip_ref,
    gain_ref,
    w_ref,
    vt,
    stat,
    acc,
    pair_out,
    pair_in,
    st_out,
    st_in,
    gt_out,
    gt,
    enter,
    reach,
    carry_out,
    carry_in,
    next_out,
    next_in,
    o_out,
    os_out,
    o_in,
    os_in,
    comb,
    prod,
    rsx,
    red_out,
    rsy,
    local_sem,
    a_send,
    a_recv,
    kv_send,
    kv_recv,
    fw_send,
    fw_recv,
    q_send,
    q_recv,
    pair_send,
    pair_recv,
    st_send,
    st_recv,
    gt_send,
    gt_recv,
    ca_send,
    ca_recv,
    o_send,
    o_recv,
    x_send,
    x_recv,
    y_send,
    y_recv,
):
    ny, nz, nx = sizes
    nh, nj = 2 * nx, 2 * nz
    tok = nh * ROWS
    half = tok // 2
    group = 2 * half
    part = 128 // nz
    scale = math.log2(math.e) / math.sqrt(HD)
    order = [0]
    for d in range(1, nz // 2 + 1):
        order += [d] if 2 * d == nz else [d, nz - d]

    c, h = lax.axis_index("ctx"), lax.axis_index("head")
    a, j = c // nj, c % nj
    z, core = j // 2, j % 2
    yh, xx = h // nx, h % nx
    sends = []

    def push(src, dst, send_sem, recv_sem, device):
        copy = pltpu.make_async_remote_copy(
            src_ref=src,
            dst_ref=dst,
            send_sem=send_sem,
            recv_sem=recv_sem,
            device_id=device,
            device_id_type=MESH,
        )
        copy.start()
        sends.append(copy)

    def landed(dst, recv_sem):
        pltpu.make_async_copy(dst, dst, recv_sem).wait()

    def at_ylo(i):
        return (((a + i) % ny) * nj + j, h)

    def at_ylo_other(i):
        return (((a + i) % ny) * nj + z * 2 + (1 - core), h)

    def at_z(d):
        return (a * nj + ((z + d) % nz) * 2 + core, h)

    def at_head(i):
        return (c, (h + i) % nh)

    def at_x(i):
        return (c, yh * nx + (xx + i) % nx)

    sibling = (a * nj + z * 2 + (1 - core), h)
    across = (c, (1 - yh) * nx + xx)

    steps_copy = pltpu.make_async_copy(steps_hbm, steps_ref, local_sem.at[3])
    steps_copy.start()
    places = [
        (slice(256, 512), lambda s: kv.at[s // nx, 0, pl.ds(pl.multiple_of((s % nx) * ROWS, ROWS), ROWS), :]),
        (slice(0, 256), lambda s: qraw.at[pl.ds(pl.multiple_of(s * ROWS, ROWS), ROWS), :]),
        (slice(512, 1024), lambda s: feat.at[pl.ds(pl.multiple_of(s * ROWS, ROWS), ROWS), :]),
    ]
    own = []
    for n, (columns, place) in enumerate(places):
        copy = pltpu.make_async_copy(x_ref.at[h, :, columns], place(h), local_sem.at[n])
        copy.start()
        own.append(copy)
    skip_copy = pltpu.make_async_copy(skip_hbm, skip_ref, local_sem.at[4])
    skip_copy.start()
    gain_copy = pltpu.make_async_copy(gain_hbm, gain_ref, local_sem.at[5])
    gain_copy.start()
    w_copy = pltpu.make_async_copy(w_hbm, w_ref, local_sem.at[6])
    w_copy.start()

    barrier = pltpu.get_barrier_semaphore()
    peers = [at_head(i) for i in range(1, nh)] + [at_z(d) for d in range(1, nz)] + [sibling]
    peers += [at_ylo(i) for i in range(1, ny)] + [at_ylo_other(i) for i in range(1, ny)]
    for peer in peers:
        pl.semaphore_signal(barrier, inc=1, device_id=peer, device_id_type=MESH)
    pl.semaphore_wait(barrier, len(peers))

    def features_out(n):
        columns, place = places[n]
        for i in range(1, nh):
            g = (h + i) % nh
            push(x_ref.at[g, :, columns], place(h), a_send.at[n, i], a_recv.at[n, i], at_head(i))

    def steps_go():
        steps_copy.wait()
        steps_out[...] = jnp.zeros((nh, 8, 128), F32)
        steps_out[:, 0:4, 0:ROWS] = steps_ref[...].astype(F32)
        for i in range(1, nh):
            push(steps_out.at[(h + i) % nh], steps_in.at[h], a_send.at[3, i], a_recv.at[3, i], at_head(i))
        steps_in[h] = steps_out[h]

    for n in LEAVE:
        if n == 3:
            steps_go()
        else:
            features_out(n)

    def rows_in(n):
        own[n].wait()
        for i in range(1, nh):
            landed(places[n][1]((h + nh - i) % nh), a_recv.at[n, i])

    halves = (yh, 1 - yh)

    def keys(n):
        if n == 0:
            own[0].wait()
        for i in range(n == 0, nx):
            s = halves[n] * nx + (xx + i) % nx
            landed(places[0][1](s), a_recv.at[0, (h + nh - s) % nh])
        mine = kv.at[halves[n], 0]
        for e in range(1, nz):
            push(mine, kv.at[halves[n], 2 * e], kv_send.at[n, e], kv_recv.at[n, e], at_z(nz - order[e]))
        push(mine, kv.at[halves[n], 1], fw_send.at[n, 0], fw_recv.at[n, 0], sibling)

    def pass_on(n, e):
        block = kv.at[halves[n], 2 * e]
        landed(block, kv_recv.at[n, e])
        push(block, kv.at[halves[n], 2 * e + 1], fw_send.at[n, e], fw_recv.at[n, e], sibling)

    def queries():
        rows_in(1)
        for i in range(2):
            for n in range(2):
                q[0, i, n * half : (n + 1) * half, :] = qraw[i * half : (i + 1) * half, n * HD : (n + 1) * HD]
        for i in range(1, ny):
            push(q.at[0], q.at[ny - i], q_send.at[i], q_recv.at[i], at_ylo(i))

    row_id = lax.broadcasted_iota(jnp.int32, (tok, tok), 0)
    col_id = lax.broadcasted_iota(jnp.int32, (tok, tok), 1)
    lower = (col_id <= row_id) & ((row_id < half) == (col_id < half))
    early_row = lax.broadcasted_iota(jnp.int32, (tok, 128), 0) < half
    first_head = lax.broadcasted_iota(jnp.int32, (tok, 128), 1) < HP
    is_early_core = core == 0
    known = {}

    def pieces():
        rows_in(2)
        for i in range(1, nh):
            landed(steps_in.at[(h + nh - i) % nh], a_recv.at[3, i])
        st_t = steps_in[0]
        for g in range(1, nh):
            st_t = st_t + pltpu.roll(steps_in[g], g * ROWS, 1)
        st_t = st_t[:, 0:tok]
        st_f = jnp.concatenate([st_t, jnp.zeros((120, tok), F32)], axis=0).T
        cum = nn_dot(jnp.where(lower, 1.0, 0.0).astype(BF16), st_f.astype(BF16))
        total_e, total_l = cum[half - 1 : half, :], cum[tok - 1 : tok, :]
        to_end = jnp.exp(jnp.where(early_row, total_e, total_l) - cum)
        weigh = jnp.where(first_head, to_end[:, 2:3] * st_f[:, 0:1], to_end[:, 3:4] * st_f[:, 1:2])
        x_in, b_in = feat[:, 0:128], feat[:, 256:384]
        xs_t = (x_in.astype(F32) * weigh).T
        early_lane = lax.broadcasted_iota(jnp.int32, (128, tok), 1) < half
        piece_e = nn_dot(jnp.where(early_lane, xs_t, 0.0).astype(BF16), b_in)
        piece_l = nn_dot(jnp.where(early_lane, 0.0, xs_t).astype(BF16), b_in)
        head_rows = lax.broadcasted_iota(jnp.int32, (128, 128), 0) < HP
        decay_e, decay_l = (
            jnp.exp(jnp.where(head_rows, t[:, 2:3], t[:, 3:4])) for t in (total_e, total_l)
        )
        pair_out[0] = jnp.where(is_early_core, piece_l, piece_e)
        pair_out[1] = jnp.where(is_early_core, decay_l, decay_e)
        push(pair_out, pair_in, pair_send.at[0], pair_recv.at[0], sibling)
        known["piece"] = jnp.where(is_early_core, piece_e, piece_l)
        known["decay"] = jnp.where(is_early_core, decay_e, decay_l)
        known["cum"], known["st_t"] = cum, st_t

    def slices():
        landed(pair_in, pair_recv.at[0])
        both = pair_in[1] * known["piece"] + pair_in[0]
        decay = pair_in[1] * known["decay"]
        st_out[:, 0:part, :] = both.reshape(nz, part, NST)
        st_out[:, part:, :] = decay.reshape(nz, part, NST)[:, 0:8, :]
        for d in range(1, nz):
            push(st_out.at[(z + d) % nz], st_in.at[z], st_send.at[d], st_recv.at[d], at_z(d))
        st_in[z] = st_out[z]

    def intra():
        x_in, b_in, c_in = feat[:, 0:128], feat[:, 256:384], feat[:, 384:512]
        cum, st_t = known["cum"], known["st_t"]
        cum_t = cum.T
        pairs = nt_dot(c_in, b_in)
        within = []
        for s in range(2):
            gap = jnp.where(lower, cum[:, 2 + s : 3 + s] - cum_t[2 + s : 3 + s, :], NEG)
            mix = jnp.exp(gap) * pairs * st_t[s : s + 1, :]
            within.append(nn_dot(mix.astype(BF16), x_in))
        skip_copy.wait()
        skip = jnp.where(first_head, skip_ref[0:1, 0:1], skip_ref[0:1, 1:2])
        known["intra"] = jnp.where(first_head, within[0], within[1]) + skip * x_in.astype(F32)

    key_row = lax.broadcasted_iota(jnp.int32, (4 * half, group), 0)
    q_tok = lax.broadcasted_iota(jnp.int32, (4 * half, group), 1) % half
    picked = [None] + [jnp.where(a + i < ny, 0, 1) for i in range(1, ny)]

    def absorb(scores, values_t, lanes, first):
        top = jnp.max(scores, axis=0, keepdims=True)
        if not first:
            before = stat[0:1, lanes]
            top = jnp.maximum(top, before)
        probs = jnp.exp2(scores * scale - top * scale)
        total = jnp.sum(probs, axis=0, keepdims=True)
        added = nn_dot(values_t, probs.astype(BF16))
        if not first:
            shrink = jnp.exp2((before - top) * scale)
            total = total + stat[1:2, lanes] * shrink
            added = added + acc[:, lanes] * shrink
        stat[0:1, lanes] = top
        stat[1:2, lanes] = total
        acc[:, lanes] = added

    def attend(n):
        first = n == 0
        slots = slice(4 * n, 4 * n + 4)
        for i in range(2):
            vt[i] = kv[i, slots, :, HD : 2 * HD].reshape(4 * half, HD).T
        keys_e = kv[0, slots, :, 0:HD].reshape(4 * half, HD)
        keys_l = kv[1, slots, :, 0:HD].reshape(4 * half, HD)
        absorb(nt_dot(keys_e, q[:, 1].reshape(ny * group, HD)), vt[0], slice(0, ny * group), first)
        for i in range(1, ny):
            s = picked[i]
            at = (ny + i - 1) * group
            keys = kv[s, slots, :, 0:HD].reshape(4 * half, HD)
            absorb(nt_dot(keys, q[i, s]), vt[s], slice(at, at + group), first)
        block = jnp.zeros((4 * half, group), jnp.int32)
        for m in range(4):
            from_z = (z + order[2 * n + m // 2]) % nz
            from_core = core if m % 2 == 0 else 1 - core
            block = jnp.where(key_row // half == m, from_z * 2 + from_core, block)
        key_tok = key_row % half
        see_e = block * half + key_tok <= j * half + q_tok
        see_l = (nj - 1 - block) * half + key_tok <= (nj - 1 - j) * half + q_tok
        at = (2 * ny - 1) * group
        absorb(jnp.where(see_e, nt_dot(keys_e, q[0, 0]), NEG), vt[0], slice(at, at + group), first)
        at = 2 * ny * group
        absorb(jnp.where(see_l, nt_dot(keys_l, q[0, 1]), NEG), vt[1], slice(at, at + group), first)

    def chunk(n):
        if n == 0:
            for i in range(1, ny):
                landed(q.at[ny - i], q_recv.at[i])
        for e in (2 * n, 2 * n + 1):
            for i in range(2):
                landed(kv.at[halves[i], 2 * e + 1], fw_recv.at[i, e])
        attend(n)

    def states_in():
        for d in range(1, nz):
            landed(st_in.at[(z + nz - d) % nz], st_recv.at[d])
        state = jnp.zeros((part, NST), F32)
        decay = jnp.ones((1, NST), F32)
        for k in range(nz):
            at = jnp.where(is_early_core, k, nz - 1 - k)
            enter[at] = state
            reach[at] = jnp.broadcast_to(decay, (8, NST))
            arrived = st_in[at]
            state = arrived[part : part + 1] * state + arrived[0:part]
            decay = arrived[part : part + 1] * decay
        gt_out[0:part, :] = state
        gt_out[part:, :] = jnp.broadcast_to(decay, (8, NST))
        for i in range(1, ny):
            push(gt_out, gt.at[core, a], gt_send.at[0, i], gt_recv.at[0, i], at_ylo(i))
            push(gt_out, gt.at[core, a], gt_send.at[1, i], gt_recv.at[1, i], at_ylo_other(i))
        push(gt_out, gt.at[core, a], gt_send.at[1, 0], gt_recv.at[1, 0], sibling)
        gt[core, a] = gt_out[...]

    def carries_out():
        for i in range(1, ny):
            landed(gt.at[core, (a + ny - i) % ny], gt_recv.at[0, i])
            landed(gt.at[1 - core, (a + ny - i) % ny], gt_recv.at[1, i])
        landed(gt.at[1 - core, a], gt_recv.at[1, 0])
        first = jnp.zeros((part, NST), F32)
        state = jnp.zeros((part, NST), F32)
        for g in range(ny):
            first = jnp.where(is_early_core & (a == g), state, first)
            state = gt[0, g, part : part + 1, :] * state + gt[0, g, 0:part, :]
        for g in reversed(range(ny)):
            first = jnp.where(jnp.logical_not(is_early_core) & (a == g), state, first)
            state = gt[1, g, part : part + 1, :] * state + gt[1, g, 0:part, :]
        for k in range(nz):
            carry_out[k] = (enter[k] + reach[k, 0:1, :] * first).astype(BF16)
        for d in range(1, nz):
            push(carry_out.at[(z + d) % nz], carry_in.at[z], ca_send.at[d], ca_recv.at[d], at_z(d))
        carry_in[z] = carry_out[z]

    def next_state():
        for d in range(1, nz):
            landed(carry_in.at[(z + nz - d) % nz], ca_recv.at[d])
        into = carry_in[...].reshape(128, NST)
        next_out[...] = (known["decay"] * into.astype(F32) + known["piece"]).astype(BF16)
        push(next_out, next_in, pair_send.at[1], pair_recv.at[1], sibling)
        return into

    steps = {"queries": queries, "pieces": pieces, "slices": slices, "intra": intra}
    steps |= {"states": states_in, "carries": carries_out}
    steps |= {f"keys{n}": functools.partial(keys, n) for n in range(2)}
    steps |= {f"pass{n}{e}": functools.partial(pass_on, n, e) for n in range(2) for e in range(1, nz)}
    steps |= {f"attend{n}": functools.partial(chunk, n) for n in range(nz // 2)}
    for name in PLAN:
        if name in steps:
            steps[name]()

    for i in range(1, ny):
        for n, at in enumerate((i * group, (ny + i - 1) * group)):
            o_out[i - 1, n] = acc[:, at : at + group].astype(BF16)
            os_out[i - 1, 2 * n : 2 * n + 2, :] = stat[0:2, at : at + group]
        os_out[i - 1, 4:8, :] = jnp.zeros((4, group), F32)
        push(os_out.at[i - 1], os_in.at[ny - i - 1], o_send.at[0, i], o_recv.at[0, i], at_ylo(i))
        push(o_out.at[i - 1], o_in.at[ny - i - 1], o_send.at[1, i], o_recv.at[1, i], at_ylo(i))

    into = next_state()
    landed(next_in, pair_recv.at[1])
    carry_e = jnp.where(is_early_core, into, next_in[...])
    carry_l = jnp.where(is_early_core, next_in[...], into)
    c_in = feat[:, 384:512]
    inter = jnp.where(early_row, nt_dot(c_in, carry_e), nt_dot(c_in, carry_l))
    cum = known["cum"]
    ssm_y = known["intra"] + inter * jnp.exp(jnp.where(first_head, cum[:, 2:3], cum[:, 3:4]))
    gate = feat[:, 128:256].astype(F32)
    gated = ssm_y * (gate / (1.0 + jnp.exp(-gate)))
    mean_sq = jnp.mean(gated * gated, axis=1, keepdims=True)
    gain_copy.wait()
    comb[:, 2 * HD : 3 * HD] = (gated * lax.rsqrt(mean_sq + 1e-05) * gain_ref[...]).astype(BF16)

    def unit(n):
        lanes = slice(n * group, (n + 1) * group)
        return stat[0:1, lanes], stat[1:2, lanes], acc[:, lanes]

    early, late = [unit(2 * ny - 1)], [unit(0), unit(2 * ny)]
    for i in range(1, ny):
        landed(os_in.at[ny - i - 1], o_recv.at[0, i])
        landed(o_in.at[ny - i - 1], o_recv.at[1, i])
    for i in range(1, ny):
        s = os_in[i - 1]
        late.append((s[0:1], s[1:2], o_in[i - 1, 0].astype(F32)))
        is_early = a + i >= ny
        other = o_in[i - 1, 1].astype(F32)
        early.append((jnp.where(is_early, s[2:3], NEG), s[3:4], other))
        late.append((jnp.where(is_early, NEG, s[2:3]), s[3:4], other))
    for n, parts in enumerate((early, late)):
        top = functools.reduce(jnp.maximum, [p[0] for p in parts])
        total, weighted = 0.0, 0.0
        for m, l, o in parts:
            w = jnp.exp2((m - top) * scale)
            total = total + w * l
            weighted = weighted + w * o
        attn = (weighted / total).T.astype(BF16)
        rows = slice(n * half, (n + 1) * half)
        comb[rows, 0:HD] = attn[0:half]
        comb[rows, HD : 2 * HD] = attn[half:]

    w_copy.wait()
    width = DOUT // CUTS

    def over_x(n, way):
        for i in range(1, nx):
            push(
                prod.at[n, halves[1 - way], (xx + i) % nx],
                rsx.at[n, nx - i - 1, way],
                x_send.at[n, way, i],
                x_recv.at[n, way, i],
                at_x(i),
            )

    def sum_over_x(n, way):
        for i in range(1, nx):
            landed(rsx.at[n, nx - i - 1, way], x_recv.at[n, way, i])
        total = prod[n, halves[1 - way], xx].astype(F32)
        for i in range(nx - 1):
            total = total + rsx[n, i, way].astype(F32)
        return total

    for n in range(CUTS):
        share = nn_dot(comb[...], w_ref[:, n * width : (n + 1) * width]).astype(BF16)
        prod[n] = share.reshape(2, nx, ROWS, width)
        over_x(n, 0)
    for n in range(CUTS):
        red_out[n] = sum_over_x(n, 0).astype(BF16)
        push(red_out.at[n], rsy.at[n], y_send.at[n], y_recv.at[n], across)
        over_x(n, 1)
    for n in range(CUTS):
        total = sum_over_x(n, 1)
        landed(rsy.at[n], y_recv.at[n])
        out_ref[:, n * width : (n + 1) * width] = (total + rsy[n].astype(F32)).astype(BF16)
    for copy in sends:
        copy.wait_send()


def make(sizes):
    ny, nz, nx = sizes
    nh, nj = 2 * nx, 2 * nz
    tok = nh * ROWS
    half = tok // 2
    group = 2 * half
    part = 128 // nz
    width = DOUT // CUTS
    units = 2 * ny + 1

    def body(streams, steps, skip_d, ssm_gain, w_out):
        x = streams.transpose(1, 0, 2)
        dma = pltpu.SemaphoreType.DMA
        scratch = dict(
            kv=pltpu.VMEM((2, 2 * nz, half, 2 * HD), BF16),
            qraw=pltpu.VMEM((tok, 2 * HD), BF16),
            q=pltpu.VMEM((ny, 2, group, HD), BF16),
            feat=pltpu.VMEM((tok, 512), BF16),
            steps_ref=pltpu.VMEM((nh, 4, ROWS), BF16),
            steps_out=pltpu.VMEM((nh, 8, 128), F32),
            steps_in=pltpu.VMEM((nh, 8, 128), F32),
            skip_ref=pltpu.VMEM((1, 2), F32),
            gain_ref=pltpu.VMEM((1, 128), F32),
            w_ref=pltpu.VMEM((3 * HD, DOUT), BF16),
            vt=pltpu.VMEM((2, HD, 4 * half), BF16),
            stat=pltpu.VMEM((8, units * group), F32),
            acc=pltpu.VMEM((HD, units * group), F32),
            pair_out=pltpu.VMEM((2, 128, NST), F32),
            pair_in=pltpu.VMEM((2, 128, NST), F32),
            st_out=pltpu.VMEM((nz, part + 8, NST), F32),
            st_in=pltpu.VMEM((nz, part + 8, NST), F32),
            gt_out=pltpu.VMEM((part + 8, NST), F32),
            gt=pltpu.VMEM((2, ny, part + 8, NST), F32),
            enter=pltpu.VMEM((nz, part, NST), F32),
            reach=pltpu.VMEM((nz, 8, NST), F32),
            carry_out=pltpu.VMEM((nz, part, NST), BF16),
            carry_in=pltpu.VMEM((nz, part, NST), BF16),
            next_out=pltpu.VMEM((128, NST), BF16),
            next_in=pltpu.VMEM((128, NST), BF16),
            o_out=pltpu.VMEM((ny - 1, 2, HD, group), BF16),
            os_out=pltpu.VMEM((ny - 1, 8, group), F32),
            o_in=pltpu.VMEM((ny - 1, 2, HD, group), BF16),
            os_in=pltpu.VMEM((ny - 1, 8, group), F32),
            comb=pltpu.VMEM((tok, 3 * HD), BF16),
            prod=pltpu.VMEM((CUTS, 2, nx, ROWS, width), BF16),
            rsx=pltpu.VMEM((CUTS, nx - 1, 2, ROWS, width), BF16),
            red_out=pltpu.VMEM((CUTS, ROWS, width), BF16),
            rsy=pltpu.VMEM((CUTS, ROWS, width), BF16),
            local_sem=dma((7,)),
            a_send=dma((4, nh)),
            a_recv=dma((4, nh)),
            kv_send=dma((2, nz)),
            kv_recv=dma((2, nz)),
            fw_send=dma((2, nz)),
            fw_recv=dma((2, nz)),
            q_send=dma((ny,)),
            q_recv=dma((ny,)),
            pair_send=dma((2,)),
            pair_recv=dma((2,)),
            st_send=dma((nz,)),
            st_recv=dma((nz,)),
            gt_send=dma((2, ny)),
            gt_recv=dma((2, ny)),
            ca_send=dma((nz,)),
            ca_recv=dma((nz,)),
            o_send=dma((2, ny)),
            o_recv=dma((2, ny)),
            x_send=dma((CUTS, 2, nx)),
            x_recv=dma((CUTS, 2, nx)),
            y_send=dma((CUTS,)),
            y_recv=dma((CUTS,)),
        )
        return pl.pallas_call(
            functools.partial(kernel, sizes),
            out_shape=jax.ShapeDtypeStruct((ROWS, DOUT), BF16),
            in_specs=[pl.BlockSpec(memory_space=pl.ANY)] + [pl.BlockSpec(memory_space=pltpu.HBM)] * 4,
            out_specs=pl.BlockSpec(memory_space=pltpu.VMEM),
            scratch_shapes=list(scratch.values()),
            compiler_params=pltpu.CompilerParams(
                collective_id=0, has_side_effects=True, vmem_limit_bytes=62 * 1024 * 1024
            ),
        )(x, steps.transpose(1, 2, 0), skip_d.reshape(1, 2), ssm_gain.reshape(1, 128), w_out)

    return body


def solution(mesh):
    return jax.shard_map(
        make((N_YLO, N_Z, N_X)),
        mesh=mesh,
        in_specs=(
            P(("ctx", "head"), None, None),
            P(("ctx", "head"), None, None),
            P("head"),
            P("head"),
            P("head", None),
        ),
        out_specs=P(("ctx", "head"), None),
        check_vma=False,
    )
```

time: 77.3 us -> 65.7 us (0.85)
  Pallas kernels: 71.6 us -> 62.2 us
  local copies, waits for them, and re-layouts: 5.42 us -> 3.32 us
    pallas_call x1, Pallas kernels: 71.6 us -> 62.2 us  [body(): pl.pallas_call(functools.partial(kernel, sizes), out_shape=jax.ShapeDtype...]
    unnamed x9 -> x2, local copies, waits for them, and re-layouts: 5.42 us -> 3.32 us
where the time goes in v2:
time: 65.7 us; the launch traced here: 65.5 us
  Pallas kernels  62.2 us (95%)
  local copies, waits for them, and re-layouts  3.32 us (5%)
    pallas_call x1, Pallas kernels, body(): pl.pallas_call(functools.partial(kernel, sizes), out_shape=jax.ShapeDtype...  62.2 us
    unnamed x2, local copies, waits for them, and re-layouts  3.32 us

profile of v2, /device:TPU:8, one launch (start us, length us, event | category | flops | bytes accessed | tf_op | source)
XLA Modules:
  0.0 65.5 jit_solution(6451826632689685441)
XLA Ops:
  0.0 1.8 %copy.8 = bf16[16,8,1024]{2,0,1:T(8,128)(2,1)} copy(bf16[16,8,1024]{2,1,0:T(8,128)(2,1)} %param.5) | data formatting | bytes 524288 | tf_op args[0]
  1.8 62.2 %shard_map.55 = bf16[16,2560]{1,0:T(8,128)(2,1)} custom-call(bf16[8,16,1024]{2,1,0:T(8,128)(2,1)} %bitcast.6, bf16[8,4,16]{2,1,0:T(4,128)(2,1)} %bitcast.7, f32[1,2]{1,0:T(1,128)} %bitcast.8, f32[1,128]{1,0:T(1,128)} %bitcast.9, bf16[384,2560]{1,0:T(8,128)(2,1)} %w_hbm.1), custom_call_target="tpu_custom_call" | custom-call | tf_op jit(solution)/shard_map/pallas_call | solution.py:583
  64.0 1.5 %copy.10 = bf16[16,2560]{1,0:T(8,128)(2,1)} copy(bf16[16,2560]{1,0:T(8,128)(2,1)} %shard_map.55) | data formatting | bytes 163840

commit v3 on v2

--- a/solution.py
+++ b/solution.py
@@ -18,13 +18,14 @@
 F32, BF16 = jnp.float32, jnp.bfloat16
 NEG = -1e30
 CUTS = 2
-LEAVE = (0, 1, 2, 3)
+TWO_STEPS = False
+LEAVE = (0, 4, 2, 1, 3)
 PLAN = (
     "keys0",
+    "pieces",
+    "slices",
     "keys1",
     "queries",
-    "pieces",
-    "slices",
     "pass01",
     "pass02",
     "pass03",
@@ -32,17 +33,17 @@
     "pass05",
     "pass06",
     "pass07",
+    "pass11",
     "intra",
-    "pass11",
     "attend0",
     "pass12",
     "pass13",
+    "states",
     "attend1",
-    "states",
     "pass14",
     "pass15",
+    "carries",
     "attend2",
-    "carries",
     "pass16",
     "pass17",
     "attend3",
@@ -59,16 +60,19 @@
 
 def kernel(
     sizes,
-    x_ref,
+    x_hbm,
     steps_hbm,
     skip_hbm,
     gain_hbm,
     w_hbm,
     out_ref,
+    x_in_ref,
+    x_ref,
     kv,
     qraw,
     q,
-    feat,
+    xb,
+    zc,
     steps_ref,
     steps_out,
     steps_in,
@@ -173,23 +177,24 @@
     sibling = (a * nj + z * 2 + (1 - core), h)
     across = (c, (1 - yh) * nx + xx)
 
-    steps_copy = pltpu.make_async_copy(steps_hbm, steps_ref, local_sem.at[3])
+    x_copy = pltpu.make_async_copy(x_hbm, x_in_ref, local_sem.at[8])
+    x_copy.start()
+    steps_copy = pltpu.make_async_copy(steps_hbm, steps_ref, local_sem.at[4])
     steps_copy.start()
+    def rows_of(ref):
+        return lambda s: ref.at[pl.ds(pl.multiple_of(s * ROWS, ROWS), ROWS), :]
+
     places = [
-        (slice(256, 512), lambda s: kv.at[s // nx, 0, pl.ds(pl.multiple_of((s % nx) * ROWS, ROWS), ROWS), :]),
-        (slice(0, 256), lambda s: qraw.at[pl.ds(pl.multiple_of(s * ROWS, ROWS), ROWS), :]),
-        (slice(512, 1024), lambda s: feat.at[pl.ds(pl.multiple_of(s * ROWS, ROWS), ROWS), :]),
+        ((256, 512), lambda s: kv.at[s // nx, 0, pl.ds(pl.multiple_of((s % nx) * ROWS, ROWS), ROWS), :]),
+        ((0, 256), rows_of(qraw)),
+        ((512, 640, 768, 896), rows_of(xb)),
+        ((640, 768, 896, 1024), rows_of(zc)),
     ]
-    own = []
-    for n, (columns, place) in enumerate(places):
-        copy = pltpu.make_async_copy(x_ref.at[h, :, columns], place(h), local_sem.at[n])
-        copy.start()
-        own.append(copy)
-    skip_copy = pltpu.make_async_copy(skip_hbm, skip_ref, local_sem.at[4])
+    skip_copy = pltpu.make_async_copy(skip_hbm, skip_ref, local_sem.at[5])
     skip_copy.start()
-    gain_copy = pltpu.make_async_copy(gain_hbm, gain_ref, local_sem.at[5])
+    gain_copy = pltpu.make_async_copy(gain_hbm, gain_ref, local_sem.at[6])
     gain_copy.start()
-    w_copy = pltpu.make_async_copy(w_hbm, w_ref, local_sem.at[6])
+    w_copy = pltpu.make_async_copy(w_hbm, w_ref, local_sem.at[7])
     w_copy.start()
 
     barrier = pltpu.get_barrier_semaphore()
@@ -197,24 +202,33 @@
     peers += [at_ylo(i) for i in range(1, ny)] + [at_ylo_other(i) for i in range(1, ny)]
     for peer in peers:
         pl.semaphore_signal(barrier, inc=1, device_id=peer, device_id_type=MESH)
+
+    x_copy.wait()
+    own = []
+    for n, (cuts, place) in enumerate(places):
+        wide = [x_in_ref[:, :, cuts[m] : cuts[m + 1]].astype(F32) for m in range(0, len(cuts), 2)]
+        for m, part_of in enumerate(wide):
+            at = m * 128
+            x_ref[n, :, :, at : at + part_of.shape[2]] = jnp.swapaxes(part_of, 0, 1).astype(BF16)
+        copy = pltpu.make_async_copy(x_ref.at[n, h], place(h), local_sem.at[n])
+        copy.start()
+        own.append(copy)
     pl.semaphore_wait(barrier, len(peers))
 
     def features_out(n):
-        columns, place = places[n]
         for i in range(1, nh):
-            g = (h + i) % nh
-            push(x_ref.at[g, :, columns], place(h), a_send.at[n, i], a_recv.at[n, i], at_head(i))
+            push(x_ref.at[n, (h + i) % nh], places[n][1](h), a_send.at[n, i], a_recv.at[n, i], at_head(i))
 
     def steps_go():
         steps_copy.wait()
         steps_out[...] = jnp.zeros((nh, 8, 128), F32)
         steps_out[:, 0:4, 0:ROWS] = steps_ref[...].astype(F32)
         for i in range(1, nh):
-            push(steps_out.at[(h + i) % nh], steps_in.at[h], a_send.at[3, i], a_recv.at[3, i], at_head(i))
+            push(steps_out.at[(h + i) % nh], steps_in.at[h], a_send.at[4, i], a_recv.at[4, i], at_head(i))
         steps_in[h] = steps_out[h]
 
     for n in LEAVE:
-        if n == 3:
+        if n == 4:
             steps_go()
         else:
             features_out(n)
@@ -234,12 +248,28 @@
             landed(places[0][1](s), a_recv.at[0, (h + nh - s) % nh])
         mine = kv.at[halves[n], 0]
         for e in range(1, nz):
-            push(mine, kv.at[halves[n], 2 * e], kv_send.at[n, e], kv_recv.at[n, e], at_z(nz - order[e]))
+            if not in_two(order[e]):
+                push(mine, kv.at[halves[n], 2 * e], kv_send.at[n, e], kv_recv.at[n, e], at_z(nz - order[e]))
         push(mine, kv.at[halves[n], 1], fw_send.at[n, 0], fw_recv.at[n, 0], sibling)
+
+    def in_two(d):
+        return TWO_STEPS and 2 < d < nz - 2
+
+    def onward(block, n, d, by):
+        e = order.index(d)
+        push(block, kv.at[halves[n], 2 * e], kv_send.at[n, e], kv_recv.at[n, e], at_z(by % nz))
 
     def pass_on(n, e):
         block = kv.at[halves[n], 2 * e]
         landed(block, kv_recv.at[n, e])
+        if order[e] == 2 and in_two(3):
+            onward(block, n, 3, -1)
+            if n == 0 and in_two(4):
+                onward(block, n, 4, -2)
+        if order[e] == nz - 2 and in_two(nz - 3):
+            onward(block, n, nz - 3, 1)
+            if n == 1 and in_two(4):
+                onward(block, n, 4, 2)
         push(block, kv.at[halves[n], 2 * e + 1], fw_send.at[n, e], fw_recv.at[n, e], sibling)
 
     def queries():
@@ -252,7 +282,8 @@
 
     row_id = lax.broadcasted_iota(jnp.int32, (tok, tok), 0)
     col_id = lax.broadcasted_iota(jnp.int32, (tok, tok), 1)
-    lower = (col_id <= row_id) & ((row_id < half) == (col_id < half))
+    same_half = (row_id < half) == (col_id < half)
+    lower, upper = (col_id <= row_id) & same_half, (row_id <= col_id) & same_half
     early_row = lax.broadcasted_iota(jnp.int32, (tok, 128), 0) < half
     first_head = lax.broadcasted_iota(jnp.int32, (tok, 128), 1) < HP
     is_early_core = core == 0
@@ -261,31 +292,32 @@
     def pieces():
         rows_in(2)
         for i in range(1, nh):
-            landed(steps_in.at[(h + nh - i) % nh], a_recv.at[3, i])
+            landed(steps_in.at[(h + nh - i) % nh], a_recv.at[4, i])
         st_t = steps_in[0]
         for g in range(1, nh):
             st_t = st_t + pltpu.roll(steps_in[g], g * ROWS, 1)
         st_t = st_t[:, 0:tok]
-        st_f = jnp.concatenate([st_t, jnp.zeros((120, tok), F32)], axis=0).T
-        cum = nn_dot(jnp.where(lower, 1.0, 0.0).astype(BF16), st_f.astype(BF16))
-        total_e, total_l = cum[half - 1 : half, :], cum[tok - 1 : tok, :]
-        to_end = jnp.exp(jnp.where(early_row, total_e, total_l) - cum)
-        weigh = jnp.where(first_head, to_end[:, 2:3] * st_f[:, 0:1], to_end[:, 3:4] * st_f[:, 1:2])
-        x_in, b_in = feat[:, 0:128], feat[:, 256:384]
-        xs_t = (x_in.astype(F32) * weigh).T
+        cum_t = nn_dot(st_t.astype(BF16), jnp.where(upper, 1.0, 0.0).astype(BF16))
+        total_e, total_l = cum_t[:, half - 1 : half], cum_t[:, tok - 1 : tok]
+        early = lax.broadcasted_iota(jnp.int32, (8, tok), 1) < half
+        to_end = jnp.exp(jnp.where(early, total_e, total_l) - cum_t)
+        x_t = xb[:, 0:128].astype(F32).T
+        first_rows = lax.broadcasted_iota(jnp.int32, (128, tok), 0) < HP
+        xs_t = x_t * jnp.where(first_rows, to_end[2:3] * st_t[0:1], to_end[3:4] * st_t[1:2])
+        b_in = xb[:, 128:256]
         early_lane = lax.broadcasted_iota(jnp.int32, (128, tok), 1) < half
         piece_e = nn_dot(jnp.where(early_lane, xs_t, 0.0).astype(BF16), b_in)
         piece_l = nn_dot(jnp.where(early_lane, 0.0, xs_t).astype(BF16), b_in)
         head_rows = lax.broadcasted_iota(jnp.int32, (128, 128), 0) < HP
         decay_e, decay_l = (
-            jnp.exp(jnp.where(head_rows, t[:, 2:3], t[:, 3:4])) for t in (total_e, total_l)
+            jnp.exp(jnp.where(head_rows, t[2:3, :], t[3:4, :])) for t in (total_e, total_l)
         )
         pair_out[0] = jnp.where(is_early_core, piece_l, piece_e)
         pair_out[1] = jnp.where(is_early_core, decay_l, decay_e)
         push(pair_out, pair_in, pair_send.at[0], pair_recv.at[0], sibling)
         known["piece"] = jnp.where(is_early_core, piece_e, piece_l)
         known["decay"] = jnp.where(is_early_core, decay_e, decay_l)
-        known["cum"], known["st_t"] = cum, st_t
+        known["cum_t"], known["st_t"] = cum_t, st_t
 
     def slices():
         landed(pair_in, pair_recv.at[0])
@@ -298,9 +330,11 @@
         st_in[z] = st_out[z]
 
     def intra():
-        x_in, b_in, c_in = feat[:, 0:128], feat[:, 256:384], feat[:, 384:512]
-        cum, st_t = known["cum"], known["st_t"]
-        cum_t = cum.T
+        rows_in(3)
+        x_in, b_in, c_in = xb[:, 0:128], xb[:, 128:256], zc[:, 128:256]
+        cum_t, st_t = known["cum_t"], known["st_t"]
+        cum = jnp.concatenate([cum_t, jnp.zeros((120, tok), F32)], axis=0).T
+        known["cum"] = cum
         pairs = nt_dot(c_in, b_in)
         within = []
         for s in range(2):
@@ -434,11 +468,11 @@
     landed(next_in, pair_recv.at[1])
     carry_e = jnp.where(is_early_core, into, next_in[...])
     carry_l = jnp.where(is_early_core, next_in[...], into)
-    c_in = feat[:, 384:512]
+    c_in = zc[:, 128:256]
     inter = jnp.where(early_row, nt_dot(c_in, carry_e), nt_dot(c_in, carry_l))
     cum = known["cum"]
     ssm_y = known["intra"] + inter * jnp.exp(jnp.where(first_head, cum[:, 2:3], cum[:, 3:4]))
-    gate = feat[:, 128:256].astype(F32)
+    gate = zc[:, 0:128].astype(F32)
     gated = ssm_y * (gate / (1.0 + jnp.exp(-gate)))
     mean_sq = jnp.mean(gated * gated, axis=1, keepdims=True)
     gain_copy.wait()
@@ -492,10 +526,16 @@
             total = total + rsx[n, i, way].astype(F32)
         return total
 
+    def project(n, way):
+        rows = pl.ds(pl.multiple_of(halves[1 - way] * half, half), half)
+        share = nn_dot(comb[rows, :], w_ref[:, n * width : (n + 1) * width]).astype(BF16)
+        prod[n, halves[1 - way]] = share.reshape(nx, ROWS, width)
+
     for n in range(CUTS):
-        share = nn_dot(comb[...], w_ref[:, n * width : (n + 1) * width]).astype(BF16)
-        prod[n] = share.reshape(2, nx, ROWS, width)
+        project(n, 0)
         over_x(n, 0)
+    for n in range(CUTS):
+        project(n, 1)
     for n in range(CUTS):
         red_out[n] = sum_over_x(n, 0).astype(BF16)
         push(red_out.at[n], rsy.at[n], y_send.at[n], y_recv.at[n], across)
@@ -519,13 +559,15 @@
     units = 2 * ny + 1
 
     def body(streams, steps, skip_d, ssm_gain, w_out):
-        x = streams.transpose(1, 0, 2)
         dma = pltpu.SemaphoreType.DMA
         scratch = dict(
+            x_in_ref=pltpu.VMEM((ROWS, nh, 1024), BF16),
+            x_ref=pltpu.VMEM((4, nh, ROWS, 256), BF16),
             kv=pltpu.VMEM((2, 2 * nz, half, 2 * HD), BF16),
             qraw=pltpu.VMEM((tok, 2 * HD), BF16),
             q=pltpu.VMEM((ny, 2, group, HD), BF16),
-            feat=pltpu.VMEM((tok, 512), BF16),
+            xb=pltpu.VMEM((tok, 256), BF16),
+            zc=pltpu.VMEM((tok, 256), BF16),
             steps_ref=pltpu.VMEM((nh, 4, ROWS), BF16),
             steps_out=pltpu.VMEM((nh, 8, 128), F32),
             steps_in=pltpu.VMEM((nh, 8, 128), F32),
@@ -556,9 +598,9 @@
             rsx=pltpu.VMEM((CUTS, nx - 1, 2, ROWS, width), BF16),
             red_out=pltpu.VMEM((CUTS, ROWS, width), BF16),
             rsy=pltpu.VMEM((CUTS, ROWS, width), BF16),
-            local_sem=dma((7,)),
-            a_send=dma((4, nh)),
-            a_recv=dma((4, nh)),
+            local_sem=dma((9,)),
+            a_send=dma((5, nh)),
+            a_recv=dma((5, nh)),
             kv_send=dma((2, nz)),
             kv_recv=dma((2, nz)),
             fw_send=dma((2, nz)),
@@ -589,7 +631,7 @@
             compiler_params=pltpu.CompilerParams(
                 collective_id=0, has_side_effects=True, vmem_limit_bytes=62 * 1024 * 1024
             ),
-        )(x, steps.transpose(1, 2, 0), skip_d.reshape(1, 2), ssm_gain.reshape(1, 128), w_out)
+        )(streams, steps.transpose(1, 2, 0), skip_d.reshape(1, 2), ssm_gain.reshape(1, 128), w_out)
 
     return body
 

time: 65.7 us -> 62.1 us (0.945)
  the two profiles are of different devices: /device:TPU:8 before, /device:TPU:24 now
where the time goes in v3:
time: 62.1 us; the launch traced here: 61.9 us
  Pallas kernels  60.4 us (97%)
  local copies, waits for them, and re-layouts  1.53 us (2%)
    pallas_call x1, Pallas kernels, body(): pl.pallas_call(functools.partial(kernel, sizes), out_shape=jax.ShapeDtype...  60.4 us
    unnamed x1, local copies, waits for them, and re-layouts  1.53 us

profile of v3, /device:TPU:24, one launch (start us, length us, event | category | flops | bytes accessed | tf_op | source)
XLA Modules:
  0.0 61.9 jit_solution(5994607035632153112)
XLA Ops:
  0.0 60.4 %shard_map.55 = bf16[16,2560]{1,0:T(8,128)(2,1)} custom-call(bf16[16,8,1024]{2,1,0:T(8,128)(2,1)} %x_hbm.1, bf16[8,4,16]{2,1,0:T(4,128)(2,1)} %bitcast.3, f32[1,2]{1,0:T(1,128)} %bitcast.4, f32[1,128]{1,0:T(1,128)} %bitcast.5, bf16[384,2560]{1,0:T(8,128)(2,1)} %w_hbm.1), custom_call_target="tpu_custom_call" | custom-call | tf_op jit(solution)/shard_map/pallas_call | solution.py:625
  60.4 1.5 %copy.7 = bf16[16,2560]{1,0:T(8,128)(2,1)} copy(bf16[16,2560]{1,0:T(8,128)(2,1)} %shard_map.55) | data formatting | bytes 163840

commit v4 on v3

--- a/solution.py
+++ b/solution.py
@@ -42,10 +42,10 @@
     "attend1",
     "pass14",
     "pass15",
-    "carries",
-    "attend2",
     "pass16",
     "pass17",
+    "attend2",
+    "carries",
     "attend3",
 )
 
@@ -334,7 +334,6 @@
         x_in, b_in, c_in = xb[:, 0:128], xb[:, 128:256], zc[:, 128:256]
         cum_t, st_t = known["cum_t"], known["st_t"]
         cum = jnp.concatenate([cum_t, jnp.zeros((120, tok), F32)], axis=0).T
-        known["cum"] = cum
         pairs = nt_dot(c_in, b_in)
         within = []
         for s in range(2):
@@ -343,7 +342,10 @@
             within.append(nn_dot(mix.astype(BF16), x_in))
         skip_copy.wait()
         skip = jnp.where(first_head, skip_ref[0:1, 0:1], skip_ref[0:1, 1:2])
-        known["intra"] = jnp.where(first_head, within[0], within[1]) + skip * x_in.astype(F32)
+        gate = zc[:, 0:128].astype(F32)
+        gate = gate / (1.0 + jnp.exp(-gate))
+        known["intra"] = (jnp.where(first_head, within[0], within[1]) + skip * x_in.astype(F32)) * gate
+        known["gain"] = jnp.exp(jnp.where(first_head, cum[:, 2:3], cum[:, 3:4])) * gate
 
     key_row = lax.broadcasted_iota(jnp.int32, (4 * half, group), 0)
     q_tok = lax.broadcasted_iota(jnp.int32, (4 * half, group), 1) % half
@@ -465,15 +467,11 @@
         push(o_out.at[i - 1], o_in.at[ny - i - 1], o_send.at[1, i], o_recv.at[1, i], at_ylo(i))
 
     into = next_state()
+    c_in = zc[:, 128:256]
+    by_own = nt_dot(c_in, into)
     landed(next_in, pair_recv.at[1])
-    carry_e = jnp.where(is_early_core, into, next_in[...])
-    carry_l = jnp.where(is_early_core, next_in[...], into)
-    c_in = zc[:, 128:256]
-    inter = jnp.where(early_row, nt_dot(c_in, carry_e), nt_dot(c_in, carry_l))
-    cum = known["cum"]
-    ssm_y = known["intra"] + inter * jnp.exp(jnp.where(first_head, cum[:, 2:3], cum[:, 3:4]))
-    gate = zc[:, 0:128].astype(F32)
-    gated = ssm_y * (gate / (1.0 + jnp.exp(-gate)))
+    inter = jnp.where(early_row == is_early_core, by_own, nt_dot(c_in, next_in[...]))
+    gated = known["intra"] + inter * known["gain"]
     mean_sq = jnp.mean(gated * gated, axis=1, keepdims=True)
     gain_copy.wait()
     comb[:, 2 * HD : 3 * HD] = (gated * lax.rsqrt(mean_sq + 1e-05) * gain_ref[...]).astype(BF16)

time: 62.1 us -> 61.9 us (level)
  no operation moved by 1% of the time
where the time goes in v4:
time: 61.9 us; the launch traced here: 61.7 us
  Pallas kernels  60.2 us (97%)
  local copies, waits for them, and re-layouts  1.53 us (2%)
    pallas_call x1, Pallas kernels, body(): pl.pallas_call(functools.partial(kernel, sizes), out_shape=jax.ShapeDtype...  60.2 us
    unnamed x1, local copies, waits for them, and re-layouts  1.53 us

profile of v4, /device:TPU:24, one launch (start us, length us, event | category | flops | bytes accessed | tf_op | source)
XLA Modules:
  0.0 61.7 jit_solution(16341284922692556005)
XLA Ops:
  0.0 60.2 %shard_map.55 = bf16[16,2560]{1,0:T(8,128)(2,1)} custom-call(bf16[16,8,1024]{2,1,0:T(8,128)(2,1)} %x_hbm.1, bf16[8,4,16]{2,1,0:T(4,128)(2,1)} %bitcast.3, f32[1,2]{1,0:T(1,128)} %bitcast.4, f32[1,128]{1,0:T(1,128)} %bitcast.5, bf16[384,2560]{1,0:T(8,128)(2,1)} %w_hbm.1), custom_call_target="tpu_custom_call" | custom-call | tf_op jit(solution)/shard_map/pallas_call | solution.py:623
  60.2 1.5 %copy.7 = bf16[16,2560]{1,0:T(8,128)(2,1)} copy(bf16[16,2560]{1,0:T(8,128)(2,1)} %shard_map.55) | data formatting | bytes 163840
